TPU v7x, 256 devices: a whole 4x4x8 slice. The times are simulated.
256 devices in a mesh: space: 32 (over y, z_hi, core), tm: 8 (over z_lo, x).
Axes of the slice: x: 4, y: 4, z: 8 (z_hi: 4, z_lo: 2; z = z_hi * 2 + z_lo), core: 2. Of those that a mesh axis runs over, the one named last changes fastest.
Arguments:
- activity: bfloat16 [2048, 256, 512], P('space', 'tm'), may hold values from 0 to 8
- footprints: bfloat16 [32, 8, 16, 4, 512], P('space'), may hold values from 0.0099487305 to 1
- traces: float32 [32, 8, 16, 256], P('space', None, None, 'tm'), may hold values from 0.1 to 2
- bg_space: float32 [2, 2048, 512], P(None, 'space'), may hold values from 0.05 to 14, as said below
- bg_time: float32 [2, 256], P(None, 'tm'), may hold values from 0.5 to 2
- block_lists: int32 [32, 8, 4], P('space'), may hold values from 0 to 71, as said below
- group_order: int32 [32, 8], P('space'), may hold values from 0 to 7, each once within a row
Outputs:
- traces_out: float32 [32, 8, 16, 256], P('space', None, None, 'tm')
- footprints_out: bfloat16 [32, 8, 16, 4, 512], P('space')
- bg_space_out: float32 [2, 2048, 512], P(None, 'space')
- bg_time_out: float32 [2, 256], P(None, 'tm')
Inputs may be any that keep to these rules, and one draw needn't show every extreme that they name: `block_lists`: the 4 entries of a group differ. Entries below 4 or from 68 on lie in a neighbouring tile; a group has at most one of them, never one outside the grid, and each such entry of a tile with both neighbours is held by exactly one of its groups. `group_order`: each tile's row holds every group number once. `bg_space`: Positive.
All inputs are finite; a program needn't handle non-finite values.
Results may differ from a plain program's by a relative error of at most 0.014.
The roundings to bfloat16 on the way count: a program that leaves them out, or rounds other values in their place, can miss the bound.
Values may be sent and summed in bfloat16 or wider, within the bound.
A program may use at most 128 MiB of HBM per device.

v0:
```python
import functools

import jax
import jax.numpy as jnp
from jax import lax
from jax.experimental import pallas as pl
from jax.experimental.pallas import tpu as pltpu
from jax.sharding import PartitionSpec as P

MESH = pl.DeviceIdType.MESH
HIGH = lax.Precision.HIGHEST
F32 = jnp.float32
BF16 = jnp.bfloat16

G = 16
NG = 8
NC = NG * G
BPG = 4
BV = 512
VB = 64
EXT = 72
FR = 32
NT = 8
ROUNDS = 2
RIDGE_TRACE = 0.01 * BPG * BV
RIDGE_FOOT = 0.1 * FR * NT


def dot(a, b, precision=None):
    return lax.dot_general(a, b, (((1,), (0,)), ((), ())), precision=precision, preferred_element_type=F32)


def dot_nt(a, b, precision=None):
    return lax.dot_general(a, b, (((1,), (1,)), ((), ())), precision=precision, preferred_element_type=F32)


def split3(x):
    hi = x.astype(BF16).astype(F32)
    rest = x - hi
    mid = rest.astype(BF16).astype(F32)
    return hi, mid, rest - mid


def halves(x):
    high = x.astype(BF16)
    return high, (x - high.astype(F32)).astype(BF16)


def lanes(rows):
    return lax.broadcasted_iota(jnp.int32, (rows, NC), 1)


def fold_diagonal(square):
    group = lanes(G) // G
    out = jnp.zeros((G, NC), F32)
    for h in range(NG):
        out = out + jnp.where(group == h, square[h * G : (h + 1) * G], 0.0)
    return out


def spread_diagonal(folded):
    group = lanes(G) // G
    return jnp.concatenate([jnp.where(group == h, folded, 0.0) for h in range(NG)], axis=0)


def inverse_blocks(folded, ridge):
    first = lanes(G) % G
    sub = lax.broadcasted_iota(jnp.int32, (G, NC), 0)
    folded = folded + jnp.where(sub == first, ridge, 0.0)
    rows = []
    for n in range(G):
        moved = folded if n == 0 else pltpu.roll(folded, NC - n, 1)
        rows.append(jnp.where(first == 0, moved, jnp.where(sub == n, 1.0, 0.0)))
    for p in range(G):
        pivot = 1.0 / rows[p][p : p + 1]
        at = sub == p
        scaled = jnp.where(at, jnp.broadcast_to(pivot, (G, NC)), rows[p] * pivot)
        for n in range(G):
            if n != p:
                rows[n] = jnp.where(at, 0.0, rows[n]) - rows[n][p : p + 1] * scaled
        rows[p] = scaled
    out = jnp.zeros((G, NC), F32)
    for n in range(G):
        moved = rows[n] if n == 0 else pltpu.roll(rows[n], n, 1)
        out = jnp.where(first == n, moved, out)
    return spread_diagonal(out)


def kernel(
    nsp, levels,
    act_hbm, f0, tr_hbm, bg_hbm, bt_hbm, bl, order,
    out_tr, out_f, out_bg, out_bt,
    act, bg0, tr0, bt0, blrow, res, pieces, foot, bgs, bts, halo_f, halo_out, halo_row, tl_in, tl_out, dr_out, dr_in, corr_out, corr_in,
    part_out, part_in, edge_in, edge_pieces, edge_out, edge_sum, frame_out, frame_in, vacc, vox, zs, btm,
    in_sem, nb_s, nb_r, tm_s, tm_r, vx_s, vx_r,
):
    loads = [
        pltpu.make_async_copy(there, here, in_sem.at[i])
        for i, (there, here) in enumerate(
            ((tr_hbm, tr0), (bt_hbm, bt0), (bg_hbm, bg0), (act_hbm, act))
        )
    ]
    for load in loads:
        load.start()
    me = lax.axis_index("tm")
    sp = lax.axis_index("space")
    left = lax.rem(sp + nsp - 1, nsp)
    right = lax.rem(sp + 1, nsp)
    peers = []
    for stride, size in levels:
        q = lax.rem(sp // stride, size)
        row = []
        for d in range(1, size):
            other = lax.rem(q + d, size)
            row.append((sp + (other - q) * stride, other))
        peers.append((q, row))

    barrier = pltpu.get_barrier_semaphore()
    count = 0
    for d in range(1, NT):
        pl.semaphore_signal(barrier, inc=1, device_id=(sp, lax.rem(me + d, NT)), device_id_type=MESH)
        count += 1
    for other in (left, right):
        pl.semaphore_signal(barrier, inc=1, device_id=(other, me), device_id_type=MESH)
        count += 1
    for _, row in peers:
        for other, _ in row:
            pl.semaphore_signal(barrier, inc=1, device_id=(other, me), device_id_type=MESH)
            count += 1

    sends = []

    def send(src, dst, ssem, rsem, device):
        copy = pltpu.make_async_remote_copy(
            src_ref=src, dst_ref=dst, send_sem=ssem, recv_sem=rsem, device_id=device, device_id_type=MESH
        )
        copy.start()
        sends.append(copy)

    def arrived(ref, ssem, rsem, device):
        pltpu.make_async_remote_copy(
            src_ref=ref, dst_ref=ref, send_sem=ssem, recv_sem=rsem, device_id=device, device_id_type=MESH
        ).wait_recv()

    def to_neighbours(cat, src_left, src_right, dst):
        send(src_right, dst(0), nb_s.at[cat, 0], nb_r.at[cat, 0], (right, me))
        send(src_left, dst(1), nb_s.at[cat, 1], nb_r.at[cat, 1], (left, me))

    def from_neighbours(cat, dst):
        arrived(dst(0), nb_s.at[cat, 0], nb_r.at[cat, 0], (left, me))
        arrived(dst(1), nb_s.at[cat, 1], nb_r.at[cat, 1], (right, me))

    def to_frames(kind, r, src, dst):
        for d in range(1, NT):
            to = lax.rem(me + d, NT)
            send(src(to), dst(me), tm_s.at[kind, r, to], tm_r.at[kind, r, me], (sp, to))

    def from_frames(kind, r, dst):
        for d in range(1, NT):
            other = lax.rem(me + d, NT)
            arrived(dst(other), tm_s.at[kind, r, other], tm_r.at[kind, r, other], (sp, other))

    def group_rows(i):
        return pl.ds(pl.multiple_of(i * G, G), G)

    entry = [[bl[k, g] for k in range(BPG)] for g in range(NG)]
    group32 = lanes(FR) // G

    for k in range(BPG):
        row = jnp.zeros((FR, NC), jnp.int32)
        for g in range(NG):
            row = jnp.where(group32 == g, entry[g][k], row)
        blrow[:, k * NC : (k + 1) * NC] = row
    halo_id = jnp.full((G, NC), -1, jnp.int32)
    halo_k, halo_any, halo_at = [], [], []
    group16 = lanes(G) // G
    for g in range(NG):
        hid = jnp.int32(-1)
        hk = jnp.int32(0)
        for k in range(BPG):
            out = jnp.logical_or(entry[g][k] < 4, entry[g][k] >= 68)
            hid = jnp.where(out, entry[g][k], hid)
            hk = jnp.where(out, k, hk)
        halo_id = jnp.where(group16 == g, hid, halo_id)
        halo_k.append(hk)
        halo_any.append(hid >= 0)
        halo_at.append(jnp.where(hid >= 68, hid - 64, jnp.maximum(hid, 0)))
    halo_bf = halo_id.astype(F32).astype(BF16)

    def stage_traces(i, low):
        tl_out[i, 0:FR, :] = low
        tl_out[i, FR : FR + G, :] = halo_bf

    def gram_of(source):
        everything = source[...].reshape(BPG * NC, BV)
        total = jnp.zeros((NC, NC), F32)
        for k in range(BPG):
            product = dot_nt(source[k], everything)
            column = jnp.concatenate([jnp.full((G, NC), entry[g][k], jnp.int32) for g in range(NG)], axis=0)
            for j in range(BPG):
                row = blrow[:, j * NC : (j + 1) * NC]
                row = jnp.concatenate([row] * (NC // FR), axis=0)
                total = total + jnp.where(column == row, product[:, j * NC : (j + 1) * NC], 0.0)
        return total

    def field(r, j):
        if r == 0:
            rows = pl.ds(pl.multiple_of(8 * j, 8), 8)
            return jnp.concatenate([bg0[0, rows, :], bg0[1, rows, :]], axis=0)
        return bgs[r - 1, j].astype(F32)

    def chunk(inst, j, source, low4, traces_i, r, side, drive):
        parts = []
        for i in range(8):
            parts.append(jnp.where(blrow[...] == 8 * j + 4 + i, low4, 0.0).astype(BF16))
        lhs = jnp.concatenate(parts, axis=0)
        rebuilt = dot(lhs, source[...].reshape(BPG * NC, BV))
        if side is not None:
            low = tl_in[traces_i, side, 0:FR, :].astype(F32)
            hid = tl_in[traces_i, side, FR : FR + G, :].astype(F32)
            hid = jnp.concatenate([hid, hid], axis=0)
            base = 68.0 if side == 0 else 0.0
            near = jnp.concatenate(
                [jnp.where(hid == base + i, low, 0.0).astype(BF16) for i in range(4)], axis=0
            )
            near = dot(near, halo_f[r, side])
            edge = slice(0, 4) if side == 0 else slice(4, 8)
            if side == 0:
                rebuilt = jnp.concatenate([rebuilt[: 4 * FR] + near, rebuilt[4 * FR :]], axis=0)
            else:
                rebuilt = jnp.concatenate([rebuilt[: 4 * FR], rebuilt[4 * FR :] + near], axis=0)
        t0 = jnp.concatenate([bts[0]] * (BV // NC), axis=1)
        t1 = jnp.concatenate([bts[1]] * (BV // NC), axis=1)
        s = field(r, j)
        s0, s1 = s[0:8], s[8:16]
        out = []
        for i in range(8):
            backdrop = s0[i : i + 1] * t0 + s1[i : i + 1] * t1
            seen = act[8 * j + i].astype(F32)
            value = ((seen - rebuilt[i * FR : (i + 1) * FR]) - backdrop).astype(BF16)
            res[inst, 8 * j + 4 + i] = value
            out.append(value)
        if side is not None and drive:
            flat = jnp.concatenate(out[edge], axis=0)
            back = dot_nt(flat, halo_f[r, side])
            total = jnp.zeros((FR, NC), F32)
            for i in range(4):
                total = total + jnp.where(hid == base + i, back[i * FR : (i + 1) * FR], 0.0)
            dr_out[r, side] = total

    def background(inst, r):
        def body(j, carry):
            flat = res[inst, pl.ds(8 * j + 4, 8)].reshape(8 * FR, BV)
            frame = dot(btm[...], flat)
            frame_out[r, j] = (frame[0:16] + frame[16:32] + frame[32:48]).astype(BF16)
            s = jnp.concatenate([x.astype(BF16) for x in split3(field(r, j))], axis=0)
            vacc[...] += dot_nt(flat, s)
            return carry

        lax.fori_loop(0, 8, body, 0)

    def middle(inst, source, low4, r, start, stop):
        def body(j, carry):
            chunk(inst, j, source, low4, None, r, None, False)
            return carry

        lax.fori_loop(start, stop, body, 0)

    def edges(inst, source, low4, traces_i, r, drive):
        chunk(inst, 0, source, low4, traces_i, r, 0, drive)
        chunk(inst, 7, source, low4, traces_i, r, 1, drive)

    def four(low):
        return jnp.concatenate([low.astype(F32)] * BPG, axis=1)

    def gather(inst):
        for g in range(NG):
            for k in range(BPG):
                pieces[k, g * FR : (g + 1) * FR, :] = res[inst, entry[g][k]]

    loads[0].wait()
    loads[1].wait()
    eye32 = jnp.where(
        lax.broadcasted_iota(jnp.int32, (FR, FR), 0) == lax.broadcasted_iota(jnp.int32, (FR, FR), 1), 1.0, 0.0
    )
    eye = jnp.where(lax.broadcasted_iota(jnp.int32, (NC, NC), 0) == lanes(NC), 1.0, 0.0)
    traces_now = dot_nt(eye32, tr0[...], HIGH)
    for c in range(2):
        bts[c] = dot_nt(eye32, jnp.broadcast_to(bt0[c : c + 1, :], (NC, FR)), HIGH)
    low = traces_now.astype(BF16)
    for g in range(NG):
        halo_out[g * G : (g + 1) * G, :] = f0[halo_k[g], g * G : (g + 1) * G, :]
    stage_traces(0, low)
    for i in range(2 * ROUNDS):
        res[i, 0:4] = jnp.zeros((4, FR, BV), BF16)
        res[i, 68:72] = jnp.zeros((4, FR, BV), BF16)

    pl.semaphore_wait(barrier, count)
    to_neighbours(0, halo_out, halo_out, lambda s: halo_f.at[0, s])
    to_neighbours(2, tl_out.at[0], tl_out.at[0], lambda s: tl_in.at[0, s])

    for r in range(ROUNDS):
        source = f0 if r == 0 else foot.at[0]
        gram = gram_of(source)
        inverse = inverse_blocks(fold_diagonal(gram), RIDGE_TRACE)
        weights = dot(gram, inverse, HIGH)

        if r == 0:
            loads[2].wait()
            loads[3].wait()
        middle(2 * r, source, four(low), r, 1, 7)
        if r == 0:
            from_neighbours(0, lambda s: halo_f.at[0, s])
            from_neighbours(2, lambda s: tl_in.at[0, s])
        else:
            for side in range(2):
                from_frames(6 + side, r - 1, lambda at, side=side: halo_f.at[r, side, group_rows(at)])
        edges(2 * r, source, four(low), r, r, True)
        to_neighbours(5 + 2 * r, dr_out.at[r, 0], dr_out.at[r, 1], lambda s: dr_in.at[r, s])
        gather(2 * r)
        cross = jnp.zeros((NG * FR, NC), F32)
        for k in range(BPG):
            cross = cross + dot_nt(pieces[k], source[k])
        drives = jnp.zeros((FR, NC), F32)
        for g in range(NG):
            drives = drives + jnp.where(group32 == g, cross[g * FR : (g + 1) * FR], 0.0)
        from_neighbours(5 + 2 * r, lambda s: dr_in.at[r, s])
        drives = drives + (dr_in[r, 0] + dr_in[r, 1])
        drives = dot(drives, inverse, HIGH)
        high, rest = halves(weights)
        weights = jnp.concatenate([high, high, rest], axis=0)
        current = traces_now
        for p in range(NG):
            high, rest = halves(current - traces_now)
            coupled = dot(jnp.concatenate([high, rest, high], axis=1), weights)
            fresh = jnp.maximum(current + (drives - coupled), 0.0)
            current = jnp.where(group32 == order[p], fresh, current)
        traces_now = current
        low = traces_now.astype(BF16)

        stage_traces(r + 1, low)
        to_neighbours(3 + r, tl_out.at[r + 1], tl_out.at[r + 1], lambda s: tl_in.at[r + 1, s])
        corr = lax.dot_general(
            traces_now, traces_now, (((0,), (0,)), ((), ())), precision=HIGH, preferred_element_type=F32
        )
        sq = [jnp.sum(bts[c] * bts[c], axis=0, keepdims=True) for c in range(2)]
        corr_out[r, 0:G, :] = fold_diagonal(corr)
        corr_out[r, G : G + 4, :] = jnp.broadcast_to(sq[0], (4, NC))
        corr_out[r, G + 4 : G + 8, :] = jnp.broadcast_to(sq[1], (4, NC))
        to_frames(0, r, lambda to: corr_out.at[r], lambda at: corr_in.at[r, at])

        inst = 2 * r + 1
        middle(inst, source, four(low), r, 1, 7)
        from_neighbours(3 + r, lambda s: tl_in.at[r + 1, s])
        edges(inst, source, four(low), r + 1, r, False)
        cat = 5 + inst
        to_neighbours(
            cat, res.at[inst, pl.ds(4, 4)], res.at[inst, pl.ds(64, 4)], lambda s: edge_in.at[r, pl.ds(4 * s, 4)]
        )

        from_frames(0, r, lambda at: corr_in.at[r, at])
        corr_in[r, me] = corr_out[r]
        total = corr_in[r, 0]
        for s in range(1, NT):
            total = total + corr_in[r, s]
        inverse_a = inverse_blocks(total[0:G], RIDGE_FOOT)
        square_time = [total[G : G + 1], total[G + 4 : G + 5]]
        masked = jnp.concatenate(
            [jnp.where(group32 == g, low.astype(F32), 0.0) for g in range(NG)], axis=0
        )
        z = dot_nt(inverse_a, masked, HIGH)
        z_high = z.astype(BF16)
        zs[0] = z_high
        zs[1] = (z - z_high.astype(F32)).astype(BF16)

        for g in range(NG):
            for k in range(BPG - 1):
                at = jnp.where(halo_k[g] <= k, entry[g][k + 1], entry[g][k])
                pieces[k, g * FR : (g + 1) * FR, :] = res[inst, at]
        for k in range(BPG - 1):
            part_out[r, k] = (dot(zs[0], pieces[k]) + dot(zs[1], pieces[k])).astype(BF16)
        to_frames(1, r, lambda to: part_out.at[r, :, group_rows(to)], lambda at: part_in.at[r, at])

        lane = lanes(FR)
        spread = jnp.zeros((FR, NC), F32)
        for c in range(2):
            for s, part in enumerate(split3(bts[c])):
                spread = jnp.where(lane // 8 == s * 2 + c, part, spread)
        stacked = jnp.concatenate(
            [jnp.where(lane % 8 == b, spread, 0.0).astype(BF16) for b in range(8)], axis=0
        )
        btm[...] = dot_nt(eye[0:48].astype(BF16), stacked).astype(BF16)
        vacc[...] = jnp.zeros_like(vacc)

        background(inst, r)
        to_frames(3, r, lambda to: frame_out.at[r, to], lambda at: frame_in.at[r, at])

        from_neighbours(cat, lambda s: edge_in.at[r, pl.ds(4 * s, 4)])
        for g in range(NG):
            block = edge_in[r, halo_at[g]]
            own = res[inst, jnp.where(halo_any[g], 4, entry[g][0])]
            edge_pieces[g * FR : (g + 1) * FR, :] = jnp.where(
                halo_any[g], block.astype(F32), own.astype(F32)
            ).astype(BF16)
        edge_out[r] = (dot(zs[0], edge_pieces[...]) + dot(zs[1], edge_pieces[...])).astype(BF16)
        to_frames(2, r, lambda to: edge_out.at[r, group_rows(to)], lambda at: edge_sum.at[r, at])

        row = lax.broadcasted_iota(jnp.int32, (FR, 48), 0)
        col = lax.broadcasted_iota(jnp.int32, (FR, 48), 1)
        summed = jnp.zeros((FR, 48), F32)
        for b in range(8):
            summed = summed + jnp.where(col % 8 == b, vacc[b * FR : (b + 1) * FR, :], 0.0)
        packed = jnp.zeros((FR, NC), F32)
        for c in range(2):
            total = jnp.sum(jnp.where((col // 8) % 2 == c, summed, 0.0), axis=1, keepdims=True)
            packed = jnp.where(lane == c, total, packed)
            squares = jnp.zeros((8, BV), F32)
            for j in range(8):
                part = field(r, j)[c * 8 : (c + 1) * 8]
                squares = squares + part * part
            squares = jnp.sum(jnp.sum(squares, axis=0, keepdims=True), axis=1, keepdims=True)
            packed = jnp.where(lane == 2 + c, squares, packed)

        def level_send(i, value):
            q, rows = peers[i]
            vox[r, i, q] = value
            for other, oq in rows:
                send(vox.at[r, i, q], vox.at[r, i, q], vx_s.at[r, i, oq], vx_r.at[r, i, q], (other, me))

        def level_sum(i):
            q, rows = peers[i]
            for other, oq in rows:
                arrived(vox.at[r, i, oq], vx_s.at[r, i, oq], vx_r.at[r, i, oq], (other, me))
            total = vox[r, i, 0]
            for s in range(1, levels[i][1]):
                total = total + vox[r, i, s]
            return total

        level_send(0, dot_nt(eye[0:8], packed, HIGH))

        frame = frame_out[r, me].astype(F32)
        from_frames(3, r, lambda at: frame_in.at[r, at])
        for d in range(1, NT):
            frame = frame + frame_in[r, lax.rem(me + d, NT)].astype(F32)
        scale = jnp.concatenate([jnp.broadcast_to(square_time[c], (8, NC)) for c in range(2)], axis=0)
        scale = jnp.concatenate([scale] * (BV // NC), axis=1)
        bgs[r, me] = jnp.maximum(field(r, me) + frame / (2.0 * scale), 0.0).astype(BF16)
        to_frames(5, r, lambda to: bgs.at[r, me], lambda at: bgs.at[r, at])
        my_rows = group_rows(me)
        total = part_out[r, :, my_rows].astype(F32)
        from_frames(1, r, lambda at: part_in.at[r, at])
        for d in range(1, NT):
            total = total + part_in[r, lax.rem(me + d, NT)].astype(F32)
        from_frames(2, r, lambda at: edge_sum.at[r, at])
        extra = edge_out[r, my_rows].astype(F32)
        for d in range(1, NT):
            extra = extra + edge_sum[r, lax.rem(me + d, NT)].astype(F32)
        which = jnp.int32(0)
        for k in range(BPG):
            mine = bl[k, me]
            which = jnp.where(jnp.logical_or(mine < 4, mine >= 68), k, which)
        for k in range(BPG):
            moved = jnp.where(which < k, total[max(k - 1, 0)], total[min(k, BPG - 2)])
            moved = jnp.where(which == k, extra, moved)
            fresh = jnp.maximum(source[k, my_rows, :].astype(F32) + moved, 0.0)
            foot[r, k, my_rows, :] = fresh.astype(BF16)
            spill = fresh if k == 0 else jnp.where(which == k, fresh, spill)
        last = r + 1 == ROUNDS
        if not last:
            halo_row[...] = spill.astype(BF16)
            to_neighbours(1, halo_row, halo_row, lambda s: halo_f.at[r + 1, s, my_rows])
        to_frames(4, r, lambda to: foot.at[r, :, my_rows], lambda at: foot.at[r, :, group_rows(at)])
        if not last:
            from_neighbours(1, lambda s: halo_f.at[r + 1, s, my_rows])
            for side in range(2):
                to_frames(
                    6 + side,
                    r,
                    lambda to, side=side: halo_f.at[r + 1, side, my_rows],
                    lambda at, side=side: halo_f.at[r + 1, side, group_rows(at)],
                )
        level_send(1, level_sum(0))
        from_frames(5, r, lambda at: bgs.at[r, at])
        from_frames(4, r, lambda at: foot.at[r, :, group_rows(at)])
        packed = level_sum(1)
        for c in range(2):
            change = packed[c : c + 1] / (2.0 * packed[2 + c : 3 + c])
            change = dot_nt(eye32, jnp.broadcast_to(change, (NC, FR)), HIGH)
            bts[c] = jnp.maximum(bts[c] + change, 0.0)

    out_tr[...] = dot_nt(eye, traces_now, HIGH)
    out_f[...] = foot[ROUNDS - 1]
    out_bg[...] = bgs[ROUNDS - 1]
    both = jnp.where(lanes(FR) == 0, bts[0], jnp.where(lanes(FR) == 1, bts[1], 0.0))
    out_bt[...] = dot_nt(eye[0:8], both, HIGH)[0:2]
    for copy in sends:
        copy.wait_send()


def solution(mesh):
    nsp = mesh.shape["space"]
    near = min(8, nsp)
    levels = ((1, near), (near, nsp // near))
    vmem = pl.BlockSpec(memory_space=pltpu.VMEM)
    far = pl.BlockSpec(memory_space=pltpu.HBM)
    smem = pl.BlockSpec(memory_space=pltpu.SMEM)

    def body(activity, footprints, traces, bg_space, bg_time, block_lists, group_order):
        f0 = footprints[0].reshape(NC, BPG, BV).transpose(1, 0, 2)
        tr0 = traces.reshape(NC, FR)
        out_tr, out_f, out_bg, out_bt = pl.pallas_call(
            functools.partial(kernel, nsp, levels),
            out_shape=(
                jax.ShapeDtypeStruct((NC, FR), F32),
                jax.ShapeDtypeStruct((BPG, NC, BV), BF16),
                jax.ShapeDtypeStruct((8, 16, BV), BF16),
                jax.ShapeDtypeStruct((2, FR), F32),
            ),
            in_specs=[far, vmem, far, far, far, smem, smem],
            out_specs=(vmem,) * 4,
            scratch_shapes=[
                pltpu.VMEM((VB, FR, BV), BF16),
                pltpu.VMEM((2, VB, BV), F32),
                pltpu.VMEM((NC, FR), F32),
                pltpu.VMEM((2, FR), F32),
                pltpu.VMEM((FR, BPG * NC), jnp.int32),
                pltpu.VMEM((2 * ROUNDS, EXT, FR, BV), BF16),
                pltpu.VMEM((BPG, NG * FR, BV), BF16),
                pltpu.VMEM((ROUNDS, BPG, NC, BV), BF16),
                pltpu.VMEM((ROUNDS, 8, 16, BV), BF16),
                pltpu.VMEM((2, FR, NC), F32),
                pltpu.VMEM((ROUNDS, 2, NC, BV), BF16),
                pltpu.VMEM((NC, BV), BF16),
                pltpu.VMEM((G, BV), BF16),
                pltpu.VMEM((ROUNDS + 1, 2, FR + G, NC), BF16),
                pltpu.VMEM((ROUNDS + 1, FR + G, NC), BF16),
                pltpu.VMEM((ROUNDS, 2, FR, NC), F32),
                pltpu.VMEM((ROUNDS, 2, FR, NC), F32),
                pltpu.VMEM((ROUNDS, G + 8, NC), F32),
                pltpu.VMEM((ROUNDS, NT, G + 8, NC), F32),
                pltpu.VMEM((ROUNDS, BPG - 1, NC, BV), BF16),
                pltpu.VMEM((ROUNDS, NT, BPG - 1, G, BV), BF16),
                pltpu.VMEM((ROUNDS, 8, FR, BV), BF16),
                pltpu.VMEM((NG * FR, BV), BF16),
                pltpu.VMEM((ROUNDS, NC, BV), BF16),
                pltpu.VMEM((ROUNDS, NT, G, BV), BF16),
                pltpu.VMEM((ROUNDS, NT, 16, BV), BF16),
                pltpu.VMEM((ROUNDS, NT, 16, BV), BF16),
                pltpu.VMEM((8 * FR, 48), F32),
                pltpu.VMEM((ROUNDS, 2, 8, 8, FR), F32),
                pltpu.VMEM((2, NC, NG * FR), BF16),
                pltpu.VMEM((48, 8 * FR), BF16),
                pltpu.SemaphoreType.DMA((4,)),
                pltpu.SemaphoreType.DMA((9, 2)),
                pltpu.SemaphoreType.DMA((9, 2)),
                pltpu.SemaphoreType.DMA((8, ROUNDS, NT)),
                pltpu.SemaphoreType.DMA((8, ROUNDS, NT)),
                pltpu.SemaphoreType.DMA((ROUNDS, 2, 8)),
                pltpu.SemaphoreType.DMA((ROUNDS, 2, 8)),
            ],
            compiler_params=pltpu.CompilerParams(
                collective_id=0, has_side_effects=True, vmem_limit_bytes=52 * 1024 * 1024
            ),
        )(activity, f0, tr0, bg_space, bg_time, block_lists[0].T, group_order[0])
        return (
            out_tr.reshape(1, NG, G, FR),
            out_f.transpose(1, 0, 2).reshape(1, NG, G, BPG, BV),
            out_bg.reshape(8, 2, 8, BV).transpose(1, 0, 2, 3).reshape(2, VB, BV).astype(F32),
            out_bt,
        )

    return jax.shard_map(
        body,
        mesh=mesh,
        in_specs=(
            P("space", "tm", None),
            P("space", None, None, None, None),
            P("space", None, None, "tm"),
            P(None, "space", None),
            P(None, "tm"),
            P("space", None, None),
            P("space", None),
        ),
        out_specs=(
            P("space", None, None, "tm"),
            P("space", None, None, None, None),
            P(None, "space", None),
            P(None, "tm"),
        ),
        check_vma=False,
    )
```

profile of v0, /device:TPU:6, one launch (start us, length us, event | category | flops | bytes accessed | tf_op | source)
XLA Modules:
  0.0 94.0 jit_solution(16239053880484650358)
XLA Ops:
  0.6 1.1 %copy.11 = bf16[1,8,16,4,512]{4,2,1,3,0:T(8,128)(2,1)S(1)} copy(bf16[1,8,16,4,512]{4,3,2,1,0:T(4,128)(2,1)} %param.8) | data formatting | bytes 1048576 | tf_op args[1]
  1.8 0.0 copy-start
  1.8 0.9 %copy-done = f32[2,64,512]{2,1,0:T(8,128)S(1)} copy-done((f32[2,64,512]{2,1,0:T(8,128)S(1)}, f32[2,64,512]{2,1,0:T(8,128)}, u32[]{:S(2)}) %copy-start) | copy-done | bytes 262168
  2.7 0.0 copy-start.1
  2.7 0.8 copy-done.1
  3.6 0.0 copy-start.2
  3.6 0.7 copy-done.2
  4.3 0.0 copy-start.3
  4.3 0.7 copy-done.3
  4.9 0.0 copy-start.4
  4.9 0.7 copy-done.4
  5.6 85.3 %shard_map.102 = (f32[128,32]{1,0:T(8,128)S(1)}, bf16[4,128,512]{2,1,0:T(8,128)(2,1)S(1)}, bf16[8,16,512]{2,1,0:T(8,128)(2,1)S(1)}, f32[2,32]{1,0:T(2,128)S(1)}) custom-call(bf16[64,32,512]{2,1,0:T(8,128)(2,1)} %act_hbm.1, bf16[4,128,512]{2,1,0:T(8,128)(2,1)S(1)} %bitcast.21, f32[128,32]{1,0:T(8,128)S(1)} %bitcast.24, f32[2,64,512]{2,1,0:T(8,128)S(1)} %copy-done, ...), custom_call_target="tpu_custom_call" | custom-call | tf_op jit(solution)/shard_map/pallas_call | solution.py:511
  90.9 1.2 %copy.13 = bf16[1,8,16,4,512]{4,3,2,1,0:T(4,128)(2,1)} copy(bf16[1,8,16,4,512]{4,2,1,3,0:T(8,128)(2,1)S(1)} %bitcast.22) | data formatting | bytes 1048576
  92.1 0.7 copy_bitcast_fusion
  92.8 0.6 copy.17
  93.5 0.6 copy.18
Async XLA Ops:
  1.8 1.0 %copy-start = (f32[2,64,512]{2,1,0:T(8,128)S(1)}, f32[2,64,512]{2,1,0:T(8,128)}, u32[]{:S(2)}) copy-start(f32[2,64,512]{2,1,0:T(8,128)} %bg_hbm.1) | copy-start | bytes 786436
  2.7 0.8 copy-start.1
  3.6 0.7 copy-start.2
  4.3 0.7 copy-start.3
  4.9 0.7 copy-start.4
where the time goes:
time: 94.5 us; the launch traced here: 94 us
  Pallas kernels  85.3 us (90%)
  local copies, waits for them, and re-layouts  7.34 us (8%)
    pallas_call x1, Pallas kernels, body(): pl.pallas_call(functools.partial(kernel, nsp, levels), out_shape=(jax.Sha...  85.3 us
    unnamed x14, local copies, waits for them, and re-layouts  7.34 us

commit v1 on v0

--- a/solution.py
+++ b/solution.py
@@ -88,16 +88,16 @@
 
 def kernel(
     nsp, levels,
-    act_hbm, f0, tr_hbm, bg_hbm, bt_hbm, bl, order,
+    act_hbm, f0, small, bg_hbm, bl,
     out_tr, out_f, out_bg, out_bt,
-    act, bg0, tr0, bt0, blrow, res, pieces, foot, bgs, bts, halo_f, halo_out, halo_row, tl_in, tl_out, dr_out, dr_in, corr_out, corr_in,
+    act, bg0, blrow, res, pieces, foot, bgs, bts, halo_f, halo_out, halo_row, tl_in, tl_out, dr_out, dr_in, corr_out, corr_in,
     part_out, part_in, edge_in, edge_pieces, edge_out, edge_sum, frame_out, frame_in, vacc, vox, zs, btm,
     in_sem, nb_s, nb_r, tm_s, tm_r, vx_s, vx_r,
 ):
     loads = [
         pltpu.make_async_copy(there, here, in_sem.at[i])
         for i, (there, here) in enumerate(
-            ((tr_hbm, tr0), (bt_hbm, bt0), (bg_hbm, bg0), (act_hbm, act))
+            ((bg_hbm, bg0), (act_hbm, act))
         )
     ]
     for load in loads:
@@ -278,15 +278,13 @@
             for k in range(BPG):
                 pieces[k, g * FR : (g + 1) * FR, :] = res[inst, entry[g][k]]
 
-    loads[0].wait()
-    loads[1].wait()
     eye32 = jnp.where(
         lax.broadcasted_iota(jnp.int32, (FR, FR), 0) == lax.broadcasted_iota(jnp.int32, (FR, FR), 1), 1.0, 0.0
     )
     eye = jnp.where(lax.broadcasted_iota(jnp.int32, (NC, NC), 0) == lanes(NC), 1.0, 0.0)
-    traces_now = dot_nt(eye32, tr0[...], HIGH)
+    traces_now = dot_nt(eye32, small[0:NC, :], HIGH)
     for c in range(2):
-        bts[c] = dot_nt(eye32, jnp.broadcast_to(bt0[c : c + 1, :], (NC, FR)), HIGH)
+        bts[c] = dot_nt(eye32, jnp.broadcast_to(small[NC + c : NC + c + 1, :], (NC, FR)), HIGH)
     low = traces_now.astype(BF16)
     for g in range(NG):
         halo_out[g * G : (g + 1) * G, :] = f0[halo_k[g], g * G : (g + 1) * G, :]
@@ -301,22 +299,28 @@
 
     for r in range(ROUNDS):
         source = f0 if r == 0 else foot.at[0]
+        def first_edges():
+            if r == 0:
+                from_neighbours(0, lambda s: halo_f.at[0, s])
+                from_neighbours(2, lambda s: tl_in.at[0, s])
+            else:
+                for side in range(2):
+                    from_frames(6 + side, r - 1, lambda at, side=side: halo_f.at[r, side, group_rows(at)])
+            edges(2 * r, source, four(low), r, r, True)
+            to_neighbours(5 + 2 * r, dr_out.at[r, 0], dr_out.at[r, 1], lambda s: dr_in.at[r, s])
+
+        if r > 0:
+            first_edges()
         gram = gram_of(source)
         inverse = inverse_blocks(fold_diagonal(gram), RIDGE_TRACE)
         weights = dot(gram, inverse, HIGH)
 
         if r == 0:
-            loads[2].wait()
-            loads[3].wait()
+            loads[0].wait()
+            loads[1].wait()
         middle(2 * r, source, four(low), r, 1, 7)
         if r == 0:
-            from_neighbours(0, lambda s: halo_f.at[0, s])
-            from_neighbours(2, lambda s: tl_in.at[0, s])
-        else:
-            for side in range(2):
-                from_frames(6 + side, r - 1, lambda at, side=side: halo_f.at[r, side, group_rows(at)])
-        edges(2 * r, source, four(low), r, r, True)
-        to_neighbours(5 + 2 * r, dr_out.at[r, 0], dr_out.at[r, 1], lambda s: dr_in.at[r, s])
+            first_edges()
         gather(2 * r)
         cross = jnp.zeros((NG * FR, NC), F32)
         for k in range(BPG):
@@ -334,7 +338,7 @@
             high, rest = halves(current - traces_now)
             coupled = dot(jnp.concatenate([high, rest, high], axis=1), weights)
             fresh = jnp.maximum(current + (drives - coupled), 0.0)
-            current = jnp.where(group32 == order[p], fresh, current)
+            current = jnp.where(group32 == bl[BPG, p], fresh, current)
         traces_now = current
         low = traces_now.astype(BF16)
 
@@ -351,6 +355,17 @@
 
         inst = 2 * r + 1
         middle(inst, source, four(low), r, 1, 7)
+        lane = lanes(FR)
+        spread = jnp.zeros((FR, NC), F32)
+        for c in range(2):
+            for s, part in enumerate(split3(bts[c])):
+                spread = jnp.where(lane // 8 == s * 2 + c, part, spread)
+        stacked = jnp.concatenate(
+            [jnp.where(lane % 8 == b, spread, 0.0).astype(BF16) for b in range(8)], axis=0
+        )
+        btm[...] = dot_nt(eye[0:48].astype(BF16), stacked).astype(BF16)
+        vacc[...] = jnp.zeros_like(vacc)
+
         from_neighbours(3 + r, lambda s: tl_in.at[r + 1, s])
         edges(inst, source, four(low), r + 1, r, False)
         cat = 5 + inst
@@ -380,17 +395,6 @@
         for k in range(BPG - 1):
             part_out[r, k] = (dot(zs[0], pieces[k]) + dot(zs[1], pieces[k])).astype(BF16)
         to_frames(1, r, lambda to: part_out.at[r, :, group_rows(to)], lambda at: part_in.at[r, at])
-
-        lane = lanes(FR)
-        spread = jnp.zeros((FR, NC), F32)
-        for c in range(2):
-            for s, part in enumerate(split3(bts[c])):
-                spread = jnp.where(lane // 8 == s * 2 + c, part, spread)
-        stacked = jnp.concatenate(
-            [jnp.where(lane % 8 == b, spread, 0.0).astype(BF16) for b in range(8)], axis=0
-        )
-        btm[...] = dot_nt(eye[0:48].astype(BF16), stacked).astype(BF16)
-        vacc[...] = jnp.zeros_like(vacc)
 
         background(inst, r)
         to_frames(3, r, lambda to: frame_out.at[r, to], lambda at: frame_in.at[r, at])
@@ -507,7 +511,8 @@
 
     def body(activity, footprints, traces, bg_space, bg_time, block_lists, group_order):
         f0 = footprints[0].reshape(NC, BPG, BV).transpose(1, 0, 2)
-        tr0 = traces.reshape(NC, FR)
+        small = jnp.concatenate([traces.reshape(NC, FR), bg_time], axis=0)
+        lists = jnp.concatenate([block_lists[0].T, group_order], axis=0)
         out_tr, out_f, out_bg, out_bt = pl.pallas_call(
             functools.partial(kernel, nsp, levels),
             out_shape=(
@@ -516,13 +521,11 @@
                 jax.ShapeDtypeStruct((8, 16, BV), BF16),
                 jax.ShapeDtypeStruct((2, FR), F32),
             ),
-            in_specs=[far, vmem, far, far, far, smem, smem],
+            in_specs=[far, vmem, vmem, far, smem],
             out_specs=(vmem,) * 4,
             scratch_shapes=[
                 pltpu.VMEM((VB, FR, BV), BF16),
                 pltpu.VMEM((2, VB, BV), F32),
-                pltpu.VMEM((NC, FR), F32),
-                pltpu.VMEM((2, FR), F32),
                 pltpu.VMEM((FR, BPG * NC), jnp.int32),
                 pltpu.VMEM((2 * ROUNDS, EXT, FR, BV), BF16),
                 pltpu.VMEM((BPG, NG * FR, BV), BF16),
@@ -550,7 +553,7 @@
                 pltpu.VMEM((ROUNDS, 2, 8, 8, FR), F32),
                 pltpu.VMEM((2, NC, NG * FR), BF16),
                 pltpu.VMEM((48, 8 * FR), BF16),
-                pltpu.SemaphoreType.DMA((4,)),
+                pltpu.SemaphoreType.DMA((2,)),
                 pltpu.SemaphoreType.DMA((9, 2)),
                 pltpu.SemaphoreType.DMA((9, 2)),
                 pltpu.SemaphoreType.DMA((8, ROUNDS, NT)),
@@ -561,7 +564,7 @@
             compiler_params=pltpu.CompilerParams(
                 collective_id=0, has_side_effects=True, vmem_limit_bytes=52 * 1024 * 1024
             ),
-        )(activity, f0, tr0, bg_space, bg_time, block_lists[0].T, group_order[0])
+        )(activity, f0, small, bg_space, lists)
         return (
             out_tr.reshape(1, NG, G, FR),
             out_f.transpose(1, 0, 2).reshape(1, NG, G, BPG, BV),

time: 94.5 us -> 91.7 us (0.970)
  local copies, waits for them, and re-layouts: 7.34 us -> 4.48 us
  other arithmetic: 0.73 us -> 2.3 us
  Pallas kernels: 85.3 us -> 84 us
    unnamed x14 -> x6, local copies, waits for them, and re-layouts: 7.34 us -> 4.48 us
    concatenate x0 -> x2, other arithmetic: none -> 1.57 us  [the longest x1 0.86 us: body(): small = jnp.concatenate([traces.reshape(NC, FR), bg_time], axis=0)]
    pallas_call x1, Pallas kernels: 85.3 us -> 84 us  [body(): pl.pallas_call(functools.partial(kernel, nsp, levels), out_shape=(jax.Sha...]
where the time goes in v1:
time: 91.7 us; the launch traced here: 91.5 us
  Pallas kernels  84 us (92%)
  local copies, waits for them, and re-layouts  4.48 us (5%)
  other arithmetic  2.3 us (3%)
    pallas_call x1, Pallas kernels, body(): pl.pallas_call(functools.partial(kernel, nsp, levels), out_shape=(jax.Sha...  84 us
    unnamed x6, local copies, waits for them, and re-layouts  4.48 us

profile of v1, /device:TPU:6, one launch (start us, length us, event | category | flops | bytes accessed | tf_op | source)
XLA Modules:
  0.0 91.5 jit_solution(17631560307625985454)
XLA Ops:
  0.6 0.7 pad_add_fusion.bl
  1.3 0.9 pad_maximum_fusion.small
  2.2 1.1 %copy.26 = bf16[1,8,16,4,512]{4,2,1,3,0:T(8,128)(2,1)S(1)} copy(bf16[1,8,16,4,512]{4,3,2,1,0:T(4,128)(2,1)} %param.8) | data formatting | bytes 1048576 | tf_op args[1]
  3.4 0.0 copy-start
  3.4 0.9 %copy-done = f32[2,64,512]{2,1,0:T(8,128)S(1)} copy-done((f32[2,64,512]{2,1,0:T(8,128)S(1)}, f32[2,64,512]{2,1,0:T(8,128)}, u32[]{:S(2)}) %copy-start) | copy-done | bytes 262168
  4.3 84.0 %shard_map.102 = (f32[128,32]{1,0:T(8,128)S(1)}, bf16[4,128,512]{2,1,0:T(8,128)(2,1)S(1)}, bf16[8,16,512]{2,1,0:T(8,128)(2,1)S(1)}, f32[2,32]{1,0:T(2,128)S(1)}) custom-call(bf16[64,32,512]{2,1,0:T(8,128)(2,1)} %act_hbm.1, bf16[4,128,512]{2,1,0:T(8,128)(2,1)S(1)} %bitcast.20, f32[130,32]{1,0:T(8,128)S(1)} %pad_maximum_fusion.small, ...), custom_call_target="tpu_custom_call" | custom-call | tf_op jit(solution)/shard_map/pallas_call | solution.py:516
  88.4 1.2 %copy.28 = bf16[1,8,16,4,512]{4,3,2,1,0:T(4,128)(2,1)} copy(bf16[1,8,16,4,512]{4,2,1,3,0:T(8,128)(2,1)S(1)} %bitcast.21) | data formatting | bytes 1048576
  89.6 0.7 copy_bitcast_fusion
  90.3 0.6 copy.32
  90.9 0.6 copy.33
Async XLA Ops:
  3.4 1.0 %copy-start = (f32[2,64,512]{2,1,0:T(8,128)S(1)}, f32[2,64,512]{2,1,0:T(8,128)}, u32[]{:S(2)}) copy-start(f32[2,64,512]{2,1,0:T(8,128)} %bg_hbm.1) | copy-start | bytes 786436

commit v2 on v1

--- a/solution.py
+++ b/solution.py
@@ -309,9 +309,9 @@
             edges(2 * r, source, four(low), r, r, True)
             to_neighbours(5 + 2 * r, dr_out.at[r, 0], dr_out.at[r, 1], lambda s: dr_in.at[r, s])
 
+        gram = gram_of(source)
         if r > 0:
             first_edges()
-        gram = gram_of(source)
         inverse = inverse_blocks(fold_diagonal(gram), RIDGE_TRACE)
         weights = dot(gram, inverse, HIGH)
 

time: 91.7 us -> 91.4 us (level)
  no operation moved by 1% of the time
where the time goes in v2:
time: 91.4 us; the launch traced here: 91.2 us
  Pallas kernels  83.7 us (92%)
  local copies, waits for them, and re-layouts  4.48 us (5%)
  other arithmetic  2.3 us (3%)
    pallas_call x1, Pallas kernels, body(): pl.pallas_call(functools.partial(kernel, nsp, levels), out_shape=(jax.Sha...  83.7 us
    unnamed x6, local copies, waits for them, and re-layouts  4.48 us

profile of v2, /device:TPU:6, one launch (start us, length us, event | category | flops | bytes accessed | tf_op | source)
XLA Modules:
  0.0 91.2 jit_solution(11905330033341951518)
XLA Ops:
  0.6 0.7 pad_add_fusion.bl
  1.3 0.9 pad_maximum_fusion.small
  2.2 1.1 %copy.26 = bf16[1,8,16,4,512]{4,2,1,3,0:T(8,128)(2,1)S(1)} copy(bf16[1,8,16,4,512]{4,3,2,1,0:T(4,128)(2,1)} %param.8) | data formatting | bytes 1048576 | tf_op args[1]
  3.4 0.0 copy-start
  3.4 0.9 %copy-done = f32[2,64,512]{2,1,0:T(8,128)S(1)} copy-done((f32[2,64,512]{2,1,0:T(8,128)S(1)}, f32[2,64,512]{2,1,0:T(8,128)}, u32[]{:S(2)}) %copy-start) | copy-done | bytes 262168
  4.3 83.7 %shard_map.102 = (f32[128,32]{1,0:T(8,128)S(1)}, bf16[4,128,512]{2,1,0:T(8,128)(2,1)S(1)}, bf16[8,16,512]{2,1,0:T(8,128)(2,1)S(1)}, f32[2,32]{1,0:T(2,128)S(1)}) custom-call(bf16[64,32,512]{2,1,0:T(8,128)(2,1)} %act_hbm.1, bf16[4,128,512]{2,1,0:T(8,128)(2,1)S(1)} %bitcast.20, f32[130,32]{1,0:T(8,128)S(1)} %pad_maximum_fusion.small, ...), custom_call_target="tpu_custom_call" | custom-call | tf_op jit(solution)/shard_map/pallas_call | solution.py:516
  88.0 1.2 %copy.28 = bf16[1,8,16,4,512]{4,3,2,1,0:T(4,128)(2,1)} copy(bf16[1,8,16,4,512]{4,2,1,3,0:T(8,128)(2,1)S(1)} %bitcast.21) | data formatting | bytes 1048576
  89.2 0.7 copy_bitcast_fusion
  90.0 0.6 copy.32
  90.6 0.6 copy.33
Async XLA Ops:
  3.4 1.0 %copy-start = (f32[2,64,512]{2,1,0:T(8,128)S(1)}, f32[2,64,512]{2,1,0:T(8,128)}, u32[]{:S(2)}) copy-start(f32[2,64,512]{2,1,0:T(8,128)} %bg_hbm.1) | copy-start | bytes 786436
